TPU v7x, 256 devices: a whole 4x4x8 slice. The times are simulated.
256 devices in a mesh: seq: 32 (over y, x, core), head: 8 (over z).
Axes of the slice: x: 4, y: 4, z: 8, core: 2. Of those that a mesh axis runs over, the one named last changes fastest.
Arguments:
- q_values: bfloat16 [65536, 4096], P('seq', 'head'), may hold values from -6 to 6
- k_values: bfloat16 [65536, 4096], P('seq', 'head'), may hold values from -6 to 6
- v_values: bfloat16 [65536, 4096], P('seq', 'head'), may hold values from -6 to 6
- q_scales: float32 [65536, 32], P('seq', 'head'), may hold values from 0.5 to 4
- k_scales: float32 [65536, 32], P('seq', 'head'), may hold values from 0.5 to 4
- v_scales: float32 [65536, 32], P('seq', 'head'), may hold values from 0.5 to 2
- conv_weight: float32 [32, 33], P('head'), may hold values from -0.9 to 0.9
Outputs:
- attended: bfloat16 [65536, 4096], P('seq', 'head')
All inputs are finite; a program needn't handle non-finite values.
Results may differ from a plain program's by a relative error of at most 0.03.
Values may be sent and summed in bfloat16 or wider, within the bound.
A program may use at most 128 MiB of HBM per device.

v0:
```python
import functools
import jax
import jax.numpy as jnp
from jax import lax
from jax.sharding import Mesh
from jax.sharding import PartitionSpec as P

HEAD_DIM = 128
LANDMARKS = 256
SWEEPS = 6
SEQ = ("seq_0", "seq_1", "seq_2")


def side_by_side(arrays, axis, dim, along):
    both = jnp.concatenate(arrays, axis=along)
    result, at, finished = (lax.all_gather(both, axis, axis=dim, tiled=True), 0, [])
    for a in arrays:
        finished.append(lax.slice_in_dim(result, at, at + a.shape[along], axis=along))
        at += a.shape[along]
    return tuple(finished)


def from_everyone(shard, axis):
    copies = jnp.broadcast_to(shard, (lax.axis_size(axis), *shard.shape))
    return lax.all_to_all(copies, axis, split_axis=0, concat_axis=0, tiled=True)


def taken_together(shard, axis):
    everything = from_everyone(shard, axis)
    return jnp.max(everything, axis=0)


def packed_total(arrays, axis):
    line, at, finished = (jnp.concatenate([a.reshape(-1) for a in arrays]), 0, [])
    total = taken_together(line, axis)
    for a in arrays:
        finished.append(total[at : at + a.size].reshape(a.shape))
        at += a.size
    return tuple(finished)


def by_axis(shard, axes):
    return functools.reduce(lax.pmax, axes, shard)


def padded_2(shard, sides, width):
    for axis, dim in sides:
        count, length = (lax.axis_size(axis), shard.shape[dim])
        up = [(i, (i + 1) % count) for i in range(count - 1)]
        down = [(j, i) for i, j in up]
        last = lax.slice_in_dim(shard, length - width, length, axis=dim)
        leading = lax.slice_in_dim(shard, 0, width, axis=dim)
        before = lax.ppermute(last, axis, up)
        after = lax.ppermute(leading, axis, down)
        shard = jnp.concatenate([before, shard, after], axis=dim)
    return shard


def dequant(value_rows, scales):
    count = scales.shape[1]
    shaped = value_rows.reshape(value_rows.shape[0], count, HEAD_DIM).astype(jnp.float32)
    return (shaped * scales[:, :, None]).astype(jnp.bfloat16)


def newton(kernel, initial, right_side):
    eye_matrix = jnp.eye(kernel.shape[0], dtype=jnp.float32)
    iterate = initial
    for sweep in range(SWEEPS):
        product = jnp.dot(kernel, iterate)
        inner_term = 7.0 * eye_matrix - product
        inner_term = 15.0 * eye_matrix - jnp.dot(product, inner_term)
        inner_term = 13.0 * eye_matrix - jnp.dot(product, inner_term)
        iterate = 0.25 * jnp.dot(iterate, inner_term)
    return jnp.dot(iterate, right_side).astype(jnp.bfloat16)


def shards(q_values, k_values, v_values, q_scales, k_scales, v_scales, conv_weight):
    tok_rows = q_values.shape[0]
    head_count = q_scales.shape[1]
    seq_count = lax.axis_size(SEQ)
    marks_here = LANDMARKS // seq_count
    segment = tok_rows // marks_here
    query_rows = dequant(q_values, q_scales)
    key_rows = dequant(k_values, k_scales)
    value_rows = dequant(v_values, v_scales)

    def means(source):
        shaped = source.reshape(marks_here, segment, head_count, HEAD_DIM).astype(jnp.float32)
        return (
            jnp.mean(shaped, axis=1).astype(jnp.bfloat16).reshape(marks_here, head_count * HEAD_DIM)
        )

    query_landmarks, key_landmarks = side_by_side((means(query_rows), means(key_rows)), SEQ, 0, 1)
    query_landmarks = query_landmarks.reshape(LANDMARKS, head_count, HEAD_DIM)
    key_landmarks = key_landmarks.reshape(LANDMARKS, head_count, HEAD_DIM)
    pseudo_inverse_factor = HEAD_DIM ** (-0.5)
    landmark_kernel = (
        jnp.einsum(
            "jvc,kvc->vjk", query_landmarks, key_landmarks, preferred_element_type=jnp.float32
        )
        * pseudo_inverse_factor
    )
    middle = jax.nn.softmax(landmark_kernel, axis=-1)
    col_top = jnp.max(jnp.sum(middle, axis=1))
    row_top = jnp.max(jnp.sum(middle, axis=2))
    col_top, row_top = packed_total((col_top, row_top), "head")
    start = jnp.swapaxes(middle, 1, 2) / (col_top * row_top)
    distant_term = (
        jnp.einsum("kli,nli->lkn", query_landmarks, key_rows, preferred_element_type=jnp.float32)
        * pseudo_inverse_factor
    )
    far_top = by_axis(jnp.max(distant_term, axis=-1), SEQ)
    weight_matrix = jnp.exp(distant_term - far_top[:, :, None])
    total = jnp.sum(weight_matrix, axis=-1)
    summed = jnp.einsum(
        "lnx,xlj->nlj",
        weight_matrix.astype(jnp.bfloat16),
        value_rows,
        preferred_element_type=jnp.float32,
    )
    total, summed = (
        lax.psum(total.astype(jnp.bfloat16), SEQ).astype(jnp.float32),
        lax.psum(summed.astype(jnp.bfloat16), SEQ).astype(jnp.float32),
    )
    reduced = summed / jnp.swapaxes(total, 0, 1)[:, :, None]
    projected_values = jax.vmap(newton, in_axes=(0, 0, 1), out_axes=1)(middle, start, reduced)
    near_scores = (
        jnp.einsum("zea,uea->ezu", query_rows, key_landmarks, preferred_element_type=jnp.float32)
        * pseudo_inverse_factor
    )
    local_term = jax.nn.softmax(near_scores, axis=-1).astype(jnp.bfloat16)
    attended = jnp.einsum(
        "kbv,vkg->bkg", local_term, projected_values, preferred_element_type=jnp.float32
    ).reshape(tok_rows, head_count * HEAD_DIM)
    flat_values = value_rows.reshape(tok_rows, head_count * HEAD_DIM)
    tap_count = conv_weight.shape[1]
    padded = padded_2(flat_values, ((SEQ, 0),), tap_count // 2)
    tap_table = jnp.repeat(conv_weight, HEAD_DIM, axis=0)
    mixed = jnp.zeros((tok_rows, head_count * HEAD_DIM), jnp.float32)
    for tap_index in range(tap_count):
        mixed = (
            mixed
            + padded[tap_index : tap_index + tok_rows].astype(jnp.float32) * tap_table[:, tap_index]
        )
    return (attended + mixed).astype(jnp.bfloat16)


def solution(mesh):
    finer = Mesh(
        mesh.devices.reshape(4, 4, 2, mesh.shape["head"]), ("seq_0", "seq_1", "seq_2", "head")
    )
    placed = (
        P(SEQ, "head"),
        P(SEQ, "head"),
        P(SEQ, "head"),
        P(SEQ, "head"),
        P(SEQ, "head"),
        P(SEQ, "head"),
        P("head", None),
    )
    return jax.shard_map(
        shards, mesh=finer, in_specs=placed, out_specs=P(SEQ, "head"), check_vma=False
    )
```

profile of v0, /device:TPU:32, one launch (start us, length us, event | category | flops | bytes accessed | tf_op | source)
XLA Modules:
  0.0 302.6 jit_solution(4559212239840184039)
XLA Ops:
  6.5 4.7 %reshape.126 = f32[8,256,4,128]{3,2,1,0:T(4,128)} reshape(bf16[2048,512]{1,0:T(8,128)(2,1)} %param.7) | data formatting | bytes 6291456 | tf_op jit(solution)/shard_map/convert_element_type | solution.py:61
  11.7 4.6 %convert_reduce_fusion.1 = f32[8,4,128]{2,1,0:T(4,128)S(1)} fusion(f32[8,256,4,128]{3,2,1,0:T(4,128)} %reshape.126, f32[8,256,4]{2,1,0:T(8,128)S(1)} %bitcast.119), kind=kLoop, calls=%fused_computation.52 | loop fusion | flops 4190208 | bytes 4243456 | tf_op jit(solution)/shard_map/reduce_sum | solution.py:90
  16.3 3.0 reshape.127
  19.6 4.4 %convert_reduce_fusion = f32[8,4,128]{2,1,0:T(4,128)S(1)} fusion(f32[8,256,4,128]{3,2,1,0:T(4,128)} %reshape.127, f32[8,256,4]{2,1,0:T(8,128)S(1)} %bitcast.120), kind=kLoop, calls=%fused_computation.50 | loop fusion | flops 4190208 | bytes 4243456 | tf_op jit(solution)/shard_map/reduce_sum | solution.py:90
  24.1 25.1 %all_gather.3 = bf16[256,1024]{1,0:T(8,128)(2,1)S(1)} all-gather(bf16[8,1024]{1,0:T(8,128)(2,1)S(1)} %pad_maximum_fusion.2), channel_id=1, replica_groups=mesh['seq_0'=4,'seq_1'=4,'seq_2'=2,'head'=8] {'seq_0','seq_1','seq_2'}, dimensions={0}, use_global_device_ids=true | all-gather | bytes 540672 | tf_op jit(solution)/shard_map/all_gather | solution.py:16
  49.3 0.8 copy.112
  50.2 1.4 fusion.169
  52.5 0.7 reduce_max.55
  53.8 1.3 pad_maximum_fusion.3
  55.7 8.6 %all-to-all-start = ((f32[8,1,2]{2,1,0:T(1,128)}), f32[8,1,2]{2,1,0:T(1,128)S(1)}, u32[]{:S(2)}, u32[]{:S(2)}) async-start(f32[8,1,2]{2,1,0:T(1,128)} %broadcast_in_dim.4), calls=%async_computation | async-start | bytes 8192 | tf_op jit(solution)/shard_map/all_to_all | solution.py:25
  64.3 4.4 %multiply_reduce_fusion = (f32[4,256]{1,0:T(4,128)S(1)}, f32[4,256,2048]{2,1,0:T(8,128)}) fusion(bf16[256,4,128]{0,2,1:T(8,128)(2,1)S(1)} %bitcast.123, f32[2048,4]{0,1:T(4,128)S(1)} %copy-done.11, bf16[2048,512]{1,0:T(8,128)(2,1)S(1)} %copy-done.4), kind=kOutput, calls=%fused_computation.34 | convolution fusion | flops 544209920 | bytes 10784768 | tf_op jit(solution)/shard_map/kli,nli->lkn/dot_general | solution.py:109
  68.7 10.2 %pmax.21 = f32[4,256]{1,0:T(4,128)S(1)} all-reduce(f32[4,256]{1,0:T(4,128)S(1)} %get-tuple-element.48), channel_id=1, replica_groups=mesh['seq_0'=4,'seq_1'=4,'seq_2'=2,'head'=8] {'seq_0'}, use_global_device_ids=true, to_apply=%region_10.0 | all-reduce | flops 1024 | bytes 8192 | tf_op jit(solution)/shard_map/pmax | solution.py:43
  78.9 8.5 %pmax.22 = f32[4,256]{1,0:T(4,128)S(1)} all-reduce(f32[4,256]{1,0:T(4,128)S(1)} %pmax.21), channel_id=1, replica_groups=mesh['seq_0'=4,'seq_1'=4,'seq_2'=2,'head'=8] {'seq_1'}, use_global_device_ids=true, to_apply=%region_11.0 | all-reduce | flops 1024 | bytes 8192 | tf_op jit(solution)/shard_map/pmax | solution.py:43
  87.5 2.5 pmax.23
  90.0 4.1 %copy.106 = f32[2048,512]{0,1:T(8,128)} copy(bf16[2048,512]{1,0:T(8,128)(2,1)} %param.9) | data formatting | bytes 6291456 | tf_op jit(solution)/shard_map/convert_element_type | solution.py:61
  94.1 2.7 multiply_convert_fusion.1
  96.8 5.9 %fusion.121 = bf16[256,4,128]{0,2,1:T(8,128)(2,1)} fusion(bf16[2048,4,128]{0,2,1:T(8,128)(2,1)S(1)} %multiply_convert_fusion.1, f32[4,256,2048]{2,1,0:T(8,128)} %get-tuple-element.49, f32[4,256]{1,0:T(4,128)S(1)} %pmax.23), kind=kOutput, calls=%fused_computation.148 | convolution fusion | flops 543293440 | bytes 10752000 | tf_op jit(solution)/shard_map/lnx,xlj->nlj/dot_general | solution.py:115
  102.9 2.1 collective-permute-start
  105.1 1.5 collective-permute-start.1
  106.6 4.4 %fusion.2 = bf16[4,256]{1,0:T(4,128)(2,1)S(1)} fusion(f32[4,256,2048]{2,1,0:T(8,128)} %get-tuple-element.49, f32[4,256]{1,0:T(4,128)S(1)} %pmax.23), kind=kLoop, calls=%fused_computation.37 | loop fusion | flops 6290432 | bytes 8394752 | tf_op jit(solution)/shard_map/reduce_sum | solution.py:114
  111.1 4.2 %fusion.16 = f32[4,2048,256]{1,2,0:T(8,128)} fusion(bf16[256,4,128]{0,2,1:T(8,128)(2,1)S(1)} %bitcast.125, f32[2048,4]{0,1:T(4,128)S(1)} %copy-done.12, bf16[2048,512]{1,0:T(8,128)(2,1)S(1)} %copy-done.5), kind=kOutput, calls=%fused_computation.56 | convolution fusion | flops 540016640 | bytes 10780672 | tf_op jit(solution)/shard_map/zea,uea->ezu/dot_general | solution.py:128
  115.6 0.7 fusion.166
  116.9 11.7 %fusion.170 = (f32[4,2048]{1,0:T(4,128)S(1)}, f32[4,2048,256]{1,2,0:T(8,128)}) fusion(f32[4,2048,256]{1,2,0:T(8,128)} %fusion.16), kind=kOutput, calls=%fused_computation.199 | output fusion | flops 8388863 | bytes 16809984 | tf_op jit(solution)/shard_map/sub | solution.py:131
  128.6 2.5 mul.490
  131.1 5.3 %copy.108 = f32[2048,512]{1,0:T(8,128)} copy(f32[2048,512]{0,1:T(8,128)} %bitcast.118) | data formatting | bytes 8388608 | tf_op jit(solution)/shard_map/mul | solution.py:62
  136.5 4.9 %multiply_convert_fusion = bf16[2048,512]{1,0:T(8,128)(2,1)} fusion(f32[2048,512]{1,0:T(8,128)} %copy.108, bf16[2048,512]{1,0:T(8,128)(2,1)} %param.9), kind=kLoop, calls=%fused_computation.45 | loop fusion | flops 3145728 | bytes 8388608 | tf_op jit(solution)/shard_map/convert_element_type | solution.py:62
  141.4 64.7 %psum.15 = bf16[256,4]{0,1:T(4,128)(2,1)S(1)} all-reduce(bf16[256,4]{0,1:T(4,128)(2,1)S(1)} %bitcast.164), channel_id=1, replica_groups=mesh['seq_0'=4,'seq_1'=4,'seq_2'=2,'head'=8] {'seq_0','seq_1','seq_2'}, use_global_device_ids=true, to_apply=%region_15.0 | all-reduce | flops 1024 | bytes 4096 | tf_op jit(solution)/shard_map/psum | solution.py:122
  206.1 0.7 fusion.168
  208.1 1.4 fusion.150
  210.0 1.8 convolution_multiply_fusion.5
  211.8 4.3 %online-softmax = f32[4,256,256]{2,1,0:T(8,128)} custom-call(f32[4,256,256]{2,1,0:T(8,128)} %copy-done, f32[4,256,256]{2,1,0:T(8,128)} %convolution_multiply_fusion.5), custom_call_target="tpu_custom_call" | custom-call | tf_op online-softmax
  216.2 2.6 fusion.77
  218.8 1.4 convolution_multiply_fusion.4
  220.2 4.3 %online-softmax.1 = f32[4,256,256]{2,1,0:T(8,128)} custom-call(f32[4,256,256]{2,1,0:T(8,128)} %copy-done, f32[4,256,256]{2,1,0:T(8,128)} %convolution_multiply_fusion.4), custom_call_target="tpu_custom_call" | custom-call | tf_op online-softmax
  224.5 2.6 fusion.86
  227.1 1.4 convolution_multiply_fusion.3
  228.5 4.3 %online-softmax.2 = f32[4,256,256]{2,1,0:T(8,128)} custom-call(f32[4,256,256]{2,1,0:T(8,128)} %copy-done, f32[4,256,256]{2,1,0:T(8,128)} %convolution_multiply_fusion.3), custom_call_target="tpu_custom_call" | custom-call | tf_op online-softmax
  232.8 2.6 fusion.95
  235.4 1.4 convolution_multiply_fusion.2
  236.8 4.3 %online-softmax.3 = f32[4,256,256]{2,1,0:T(8,128)} custom-call(f32[4,256,256]{2,1,0:T(8,128)} %copy-done, f32[4,256,256]{2,1,0:T(8,128)} %convolution_multiply_fusion.2), custom_call_target="tpu_custom_call" | custom-call | tf_op online-softmax
  241.1 2.6 fusion.104
  243.7 1.4 convolution_multiply_fusion.1
  245.1 4.3 %online-softmax.4 = f32[4,256,256]{2,1,0:T(8,128)} custom-call(f32[4,256,256]{2,1,0:T(8,128)} %copy-done, f32[4,256,256]{2,1,0:T(8,128)} %convolution_multiply_fusion.1), custom_call_target="tpu_custom_call" | custom-call | tf_op online-softmax
  249.5 2.6 fusion.113
  252.1 1.4 fusion.124
  253.5 6.3 %fusion.13 = f32[4,128,2048]{2,1,0:T(8,128)} fusion(bf16[256,4,128]{2,0,1:T(8,128)(2,1)S(1)} %fusion.124, f32[4,2048,256]{1,2,0:T(8,128)} %get-tuple-element.51, f32[4,2048]{1,0:T(4,128)S(1)} %get-tuple-element.50), kind=kOutput, calls=%fused_computation.54 | convolution fusion | flops 541065216 | bytes 12877824 | tf_op jit(solution)/shard_map/kbv,vkg->bkg/dot_general | solution.py:132
  260.0 5.5 %copy.94 = f32[2048,512]{1,0:T(8,128)} copy(f32[2048,512]{0,1:T(8,128)} %bitcast.121) | data formatting | bytes 8388608 | tf_op jit(solution)/shard_map/reshape | solution.py:134
  265.9 29.8 %add_convert_fusion = bf16[2048,512]{1,0:T(8,128)(2,1)} fusion(f32[2048,512]{1,0:T(8,128)} %copy.94, bf16[2048,512]{1,0:T(8,128)(2,1)S(1)} %copy-done.6, bf16[16,512]{1,0:T(8,128)(2,1)S(1)} %collective-permute-done.1, bf16[16,512]{1,0:T(8,128)(2,1)S(1)} %collective-permute-done, f32[512]{0:T(512)S(1)} %bitcast.132, f32[512]{0:T(512)S(1)} %bitcast.133, ...), kind=kLoop, calls=%fused_computation.44 | loop fusion | flops 205520896 | bytes 8488960 | tf_op jit(solution)/shard_map/convert_element_type | solution.py:145
  (124 shorter events, 5.0 us)
Async XLA Ops:
  6.5 4.7 %copy-start.12 = (f32[2048,4]{0,1:T(4,128)S(1)}, f32[2048,4]{0,1:T(4,128)}, u32[]{:S(2)}) copy-start(f32[2048,4]{0,1:T(4,128)} %param.10) | copy-start | bytes 98308
  11.3 5.0 %copy-start.4 = (bf16[2048,512]{1,0:T(8,128)(2,1)S(1)}, bf16[2048,512]{1,0:T(8,128)(2,1)}, u32[]{:S(2)}) copy-start(bf16[2048,512]{1,0:T(8,128)(2,1)} %param.8) | copy-start | bytes 6291460
  51.6 158.4 %copy-start = (f32[4,256,256]{2,1,0:T(8,128)}, f32[4,256,256]{2,1,0:T(8,128)S(1)}, u32[]{:S(2)}) copy-start(f32[4,256,256]{2,1,0:T(8,128)S(1)} %get-tuple-element.47) | copy-start | bytes 3145732
  55.7 150.4 %all-to-all-start = ((f32[8,1,2]{2,1,0:T(1,128)}), f32[8,1,2]{2,1,0:T(1,128)S(1)}, u32[]{:S(2)}, u32[]{:S(2)}) async-start(f32[8,1,2]{2,1,0:T(1,128)} %broadcast_in_dim.4), calls=%async_computation | async-start | bytes 8192 | tf_op jit(solution)/shard_map/all_to_all | solution.py:25
  64.3 187.8 %all-reduce.2.cloned.1.call-start = ((), (), s32[]{:S(2)}) async-start(), calls=%async_computation.1 | async-start | bytes 524288 | tf_op jit(solution)/shard_map/psum | solution.py:123
  68.7 25.4 %copy-start.10 = (f32[2048,4]{0,1:T(4,128)S(1)}, f32[2048,4]{0,1:T(4,128)}, u32[]{:S(2)}) copy-start(f32[2048,4]{0,1:T(4,128)} %param.12) | copy-start | bytes 98308
  102.9 162.7 %collective-permute-start = (bf16[16,512]{1,0:T(8,128)(2,1)S(1)}, bf16[16,512]{1,0:T(8,128)(2,1)S(1)}, u32[]{:S(2)}, u32[]{:S(2)}) collective-permute-start(bf16[16,512]{1,0:T(8,128)(2,1)S(1)} %copy.107), channel_id=1, source_target_pairs={{0,8},{8,16},{16,24},{24,32},{32,40},{40,48},{48,56},{56,64},{64,7... | collective-permute-start | bytes 49160 | tf_op jit(solution)/shard_map/ppermute | solution.py:53
  105.1 160.5 %collective-permute-start.1 = (bf16[16,512]{1,0:T(8,128)(2,1)S(1)}, bf16[16,512]{1,0:T(8,128)(2,1)S(1)}, u32[]{:S(2)}, u32[]{:S(2)}) collective-permute-start(bf16[16,512]{1,0:T(8,128)(2,1)S(1)} %copy.109), channel_id=1, source_target_pairs={{8,0},{16,8},{24,16},{32,24},{40,32},{48,40},{56,48},{64,56},{72,6... | collective-permute-start | bytes 49160 | tf_op jit(solution)/shard_map/ppermute | solution.py:54
  106.6 4.5 %copy-start.5 = (bf16[2048,512]{1,0:T(8,128)(2,1)S(1)}, bf16[2048,512]{1,0:T(8,128)(2,1)}, u32[]{:S(2)}) copy-start(bf16[2048,512]{1,0:T(8,128)(2,1)} %param.7) | copy-start | bytes 6291460
  106.6 4.5 %copy-start.9 = (bf16[256,512]{0,1:T(8,128)(2,1)S(1)}, bf16[256,512]{0,1:T(8,128)(2,1)}, u32[]{:S(2)}) copy-start(bf16[256,512]{0,1:T(8,128)(2,1)} %copy.112) | copy-start | bytes 786436
  211.8 6.9 %copy-start.8 = (f32[4,256,256]{2,1,0:T(8,128)S(1)}, f32[4,256,256]{2,1,0:T(8,128)}, u32[]{:S(2)}) copy-start(f32[4,256,256]{2,1,0:T(8,128)} %convolution_multiply_fusion.5) | copy-start | bytes 3145732
  220.2 6.9 %copy-start.1 = (f32[4,256,256]{2,1,0:T(8,128)S(1)}, f32[4,256,256]{2,1,0:T(8,128)}, u32[]{:S(2)}) copy-start(f32[4,256,256]{2,1,0:T(8,128)} %convolution_multiply_fusion.4) | copy-start | bytes 3145732
  228.5 6.9 %copy-start.2 = (f32[4,256,256]{2,1,0:T(8,128)S(1)}, f32[4,256,256]{2,1,0:T(8,128)}, u32[]{:S(2)}) copy-start(f32[4,256,256]{2,1,0:T(8,128)} %convolution_multiply_fusion.3) | copy-start | bytes 3145732
  236.8 6.9 %copy-start.3 = (f32[4,256,256]{2,1,0:T(8,128)S(1)}, f32[4,256,256]{2,1,0:T(8,128)}, u32[]{:S(2)}) copy-start(f32[4,256,256]{2,1,0:T(8,128)} %convolution_multiply_fusion.2) | copy-start | bytes 3145732
  245.1 7.0 %copy-start.7 = (f32[4,256,256]{2,1,0:T(8,128)S(1)}, f32[4,256,256]{2,1,0:T(8,128)}, u32[]{:S(2)}) copy-start(f32[4,256,256]{2,1,0:T(8,128)} %convolution_multiply_fusion.1) | copy-start | bytes 3145732
  259.7 5.8 %copy-start.6 = (bf16[2048,512]{1,0:T(8,128)(2,1)S(1)}, bf16[2048,512]{1,0:T(8,128)(2,1)}, u32[]{:S(2)}) copy-start(bf16[2048,512]{1,0:T(8,128)(2,1)} %multiply_convert_fusion) | copy-start | bytes 6291460
  259.7 5.8 %copy-start.13 = (f32[512,1]{0,1:T(1,128)S(1)}, f32[512,1]{0,1:T(1,128)}, u32[]{:S(2)}) copy-start(f32[512,1]{0,1:T(1,128)} %get-tuple-element.12) | copy-start | bytes 6148
  259.7 5.8 %copy-start.14 = (f32[512,1]{0,1:T(1,128)S(1)}, f32[512,1]{0,1:T(1,128)}, u32[]{:S(2)}) copy-start(f32[512,1]{0,1:T(1,128)} %get-tuple-element.13) | copy-start | bytes 6148
  259.7 5.8 %copy-start.15 = (f32[512,1]{0,1:T(1,128)S(1)}, f32[512,1]{0,1:T(1,128)}, u32[]{:S(2)}) copy-start(f32[512,1]{0,1:T(1,128)} %get-tuple-element.14) | copy-start | bytes 6148
  259.8 5.9 %copy-start.16 = (f32[512,1]{0,1:T(1,128)S(1)}, f32[512,1]{0,1:T(1,128)}, u32[]{:S(2)}) copy-start(f32[512,1]{0,1:T(1,128)} %get-tuple-element.15) | copy-start | bytes 6148
  259.8 5.9 %copy-start.17 = (f32[512,1]{0,1:T(1,128)S(1)}, f32[512,1]{0,1:T(1,128)}, u32[]{:S(2)}) copy-start(f32[512,1]{0,1:T(1,128)} %get-tuple-element.16) | copy-start | bytes 6148
  259.8 5.9 %copy-start.18 = (f32[512,1]{0,1:T(1,128)S(1)}, f32[512,1]{0,1:T(1,128)}, u32[]{:S(2)}) copy-start(f32[512,1]{0,1:T(1,128)} %get-tuple-element.17) | copy-start | bytes 6148
  259.8 5.9 %copy-start.19 = (f32[512,1]{0,1:T(1,128)S(1)}, f32[512,1]{0,1:T(1,128)}, u32[]{:S(2)}) copy-start(f32[512,1]{0,1:T(1,128)} %get-tuple-element.18) | copy-start | bytes 6148
  259.8 5.9 %copy-start.20 = (f32[512,1]{0,1:T(1,128)S(1)}, f32[512,1]{0,1:T(1,128)}, u32[]{:S(2)}) copy-start(f32[512,1]{0,1:T(1,128)} %get-tuple-element.19) | copy-start | bytes 6148
  259.8 5.9 %copy-start.21 = (f32[512,1]{0,1:T(1,128)S(1)}, f32[512,1]{0,1:T(1,128)}, u32[]{:S(2)}) copy-start(f32[512,1]{0,1:T(1,128)} %get-tuple-element.20) | copy-start | bytes 6148
  259.8 5.9 %copy-start.22 = (f32[512,1]{0,1:T(1,128)S(1)}, f32[512,1]{0,1:T(1,128)}, u32[]{:S(2)}) copy-start(f32[512,1]{0,1:T(1,128)} %get-tuple-element.21) | copy-start | bytes 6148
  259.8 5.9 %copy-start.23 = (f32[512,1]{0,1:T(1,128)S(1)}, f32[512,1]{0,1:T(1,128)}, u32[]{:S(2)}) copy-start(f32[512,1]{0,1:T(1,128)} %get-tuple-element.22) | copy-start | bytes 6148
  259.8 5.9 %copy-start.24 = (f32[512,1]{0,1:T(1,128)S(1)}, f32[512,1]{0,1:T(1,128)}, u32[]{:S(2)}) copy-start(f32[512,1]{0,1:T(1,128)} %get-tuple-element.23) | copy-start | bytes 6148
  259.8 5.9 %copy-start.25 = (f32[512,1]{0,1:T(1,128)S(1)}, f32[512,1]{0,1:T(1,128)}, u32[]{:S(2)}) copy-start(f32[512,1]{0,1:T(1,128)} %get-tuple-element.24) | copy-start | bytes 6148
  259.9 5.9 %copy-start.26 = (f32[512,1]{0,1:T(1,128)S(1)}, f32[512,1]{0,1:T(1,128)}, u32[]{:S(2)}) copy-start(f32[512,1]{0,1:T(1,128)} %get-tuple-element.25) | copy-start | bytes 6148
  259.9 5.9 %copy-start.27 = (f32[512,1]{0,1:T(1,128)S(1)}, f32[512,1]{0,1:T(1,128)}, u32[]{:S(2)}) copy-start(f32[512,1]{0,1:T(1,128)} %get-tuple-element.26) | copy-start | bytes 6148
  259.9 5.9 %copy-start.28 = (f32[512,1]{0,1:T(1,128)S(1)}, f32[512,1]{0,1:T(1,128)}, u32[]{:S(2)}) copy-start(f32[512,1]{0,1:T(1,128)} %get-tuple-element.27) | copy-start | bytes 6148
  259.9 5.9 %copy-start.29 = (f32[512,1]{0,1:T(1,128)S(1)}, f32[512,1]{0,1:T(1,128)}, u32[]{:S(2)}) copy-start(f32[512,1]{0,1:T(1,128)} %get-tuple-element.28) | copy-start | bytes 6148
  259.9 5.9 %copy-start.30 = (f32[512,1]{0,1:T(1,128)S(1)}, f32[512,1]{0,1:T(1,128)}, u32[]{:S(2)}) copy-start(f32[512,1]{0,1:T(1,128)} %get-tuple-element.29) | copy-start | bytes 6148
  259.9 5.9 %copy-start.31 = (f32[512,1]{0,1:T(1,128)S(1)}, f32[512,1]{0,1:T(1,128)}, u32[]{:S(2)}) copy-start(f32[512,1]{0,1:T(1,128)} %get-tuple-element.30) | copy-start | bytes 6148
  259.9 5.9 %copy-start.32 = (f32[512,1]{0,1:T(1,128)S(1)}, f32[512,1]{0,1:T(1,128)}, u32[]{:S(2)}) copy-start(f32[512,1]{0,1:T(1,128)} %get-tuple-element.31) | copy-start | bytes 6148
  259.9 5.9 %copy-start.33 = (f32[512,1]{0,1:T(1,128)S(1)}, f32[512,1]{0,1:T(1,128)}, u32[]{:S(2)}) copy-start(f32[512,1]{0,1:T(1,128)} %get-tuple-element.32) | copy-start | bytes 6148
  259.9 5.9 %copy-start.34 = (f32[512,1]{0,1:T(1,128)S(1)}, f32[512,1]{0,1:T(1,128)}, u32[]{:S(2)}) copy-start(f32[512,1]{0,1:T(1,128)} %get-tuple-element.33) | copy-start | bytes 6148
  259.9 5.9 %copy-start.35 = (f32[512,1]{0,1:T(1,128)S(1)}, f32[512,1]{0,1:T(1,128)}, u32[]{:S(2)}) copy-start(f32[512,1]{0,1:T(1,128)} %get-tuple-element.34) | copy-start | bytes 6148
  259.9 5.9 %copy-start.36 = (f32[512,1]{0,1:T(1,128)S(1)}, f32[512,1]{0,1:T(1,128)}, u32[]{:S(2)}) copy-start(f32[512,1]{0,1:T(1,128)} %get-tuple-element.35) | copy-start | bytes 6148
  260.0 5.9 %copy-start.37 = (f32[512,1]{0,1:T(1,128)S(1)}, f32[512,1]{0,1:T(1,128)}, u32[]{:S(2)}) copy-start(f32[512,1]{0,1:T(1,128)} %get-tuple-element.36) | copy-start | bytes 6148
  260.0 5.9 %copy-start.38 = (f32[512,1]{0,1:T(1,128)S(1)}, f32[512,1]{0,1:T(1,128)}, u32[]{:S(2)}) copy-start(f32[512,1]{0,1:T(1,128)} %get-tuple-element.37) | copy-start | bytes 6148
  260.0 5.9 %copy-start.39 = (f32[512,1]{0,1:T(1,128)S(1)}, f32[512,1]{0,1:T(1,128)}, u32[]{:S(2)}) copy-start(f32[512,1]{0,1:T(1,128)} %get-tuple-element.38) | copy-start | bytes 6148
  260.0 5.9 %copy-start.40 = (f32[512,1]{0,1:T(1,128)S(1)}, f32[512,1]{0,1:T(1,128)}, u32[]{:S(2)}) copy-start(f32[512,1]{0,1:T(1,128)} %get-tuple-element.39) | copy-start | bytes 6148
  260.0 5.9 %copy-start.41 = (f32[512,1]{0,1:T(1,128)S(1)}, f32[512,1]{0,1:T(1,128)}, u32[]{:S(2)}) copy-start(f32[512,1]{0,1:T(1,128)} %get-tuple-element.40) | copy-start | bytes 6148
  260.0 5.9 %copy-start.42 = (f32[512,1]{0,1:T(1,128)S(1)}, f32[512,1]{0,1:T(1,128)}, u32[]{:S(2)}) copy-start(f32[512,1]{0,1:T(1,128)} %get-tuple-element.41) | copy-start | bytes 6148
  260.0 5.9 %copy-start.43 = (f32[512,1]{0,1:T(1,128)S(1)}, f32[512,1]{0,1:T(1,128)}, u32[]{:S(2)}) copy-start(f32[512,1]{0,1:T(1,128)} %get-tuple-element.42) | copy-start | bytes 6148
  260.0 5.9 %copy-start.44 = (f32[512,1]{0,1:T(1,128)S(1)}, f32[512,1]{0,1:T(1,128)}, u32[]{:S(2)}) copy-start(f32[512,1]{0,1:T(1,128)} %get-tuple-element.43) | copy-start | bytes 6148
  (2 other events, 7.3 us)
Sparse Core Ops, SparseCore 0:
  102.8 108.5 all-reduce.1
where the time goes:
time: 304 us; the launch traced here: 303 us
  blocking collectives  111 us (37%)
  other arithmetic  66.2 us (22%)
  matrix products  45.7 us (15%)
  local copies, waits for them, and re-layouts  30.2 us (10%)
  Pallas kernels  21.7 us (7%)
  between operations  15.5 us (5%)
  starting transfers between devices  12.1 us (4%)
    psum x1, blocking collectives, shards(): lax.psum(total.astype(jnp.bfloat16), SEQ).astype(jnp.float32)  64.7 us
    convert_element_type x1, other arithmetic, shards(): return (attended + mixed).astype(jnp.bfloat16)  29.8 us
    all_gather x1, blocking collectives, side_by_side(): lax.all_gather(both, axis, axis=dim, tiled=True)  25.1 us
    unnamed x5, Pallas kernels  21.7 us
    pmax x3, blocking collectives, by_axis(): return functools.reduce(lax.pmax, axes, shard)  21.3 us
    dot_general x6, matrix products, newton(): inner_term = 13.0 * eye_matrix - jnp.dot(product, inner_term)  13.4 us
    convert_element_type x3, local copies, waits for them, and re-layouts, dequant(): value_rows.reshape(value_rows.shape[0], count, HEAD_DIM).astype(jnp.float32)  11.9 us
    sub x1, other arithmetic, shards(): local_term = jax.nn.softmax(near_scores, axis=-1).astype(jnp.bfloat16)  11.7 us
  transfers between devices with their start and end apart: 4, of which 0 were waited for; matrix products, arithmetic and copies ran while one was open for 29% of the time, Pallas kernels for 7%

commit v1 on v0

--- a/solution.py
+++ b/solution.py
@@ -118,8 +118,9 @@
         value_rows,
         preferred_element_type=jnp.float32,
     )
+    define_side = lambda sheet: jnp.sum(lax.all_gather(sheet, SEQ), axis=0)
     total, summed = (
-        lax.psum(total.astype(jnp.bfloat16), SEQ).astype(jnp.float32),
+        define_side(total.astype(jnp.bfloat16)).astype(jnp.float32),
         lax.psum(summed.astype(jnp.bfloat16), SEQ).astype(jnp.float32),
     )
     reduced = summed / jnp.swapaxes(total, 0, 1)[:, :, None]

time: 304 us -> 267 us (0.88)
  blocking collectives: 111 us -> 73.2 us
    psum x1 -> x0, blocking collectives: 64.7 us -> none  [shards(): lax.psum(total.astype(jnp.bfloat16), SEQ).astype(jnp.float32)]
    all_gather x0 -> x1, blocking collectives: none -> 26.8 us  [shards(): define_side = lambda sheet: jnp.sum(lax.all_gather(sheet, SEQ), axis=0)]
  transfers between devices with their start and end apart: 4 -> 4, of which waited for: 0 -> 0; matrix products, arithmetic and copies ran while one was open for 29% -> 33% of each run, Pallas kernels for 7% -> 8%
where the time goes in v1:
time: 267 us; the launch traced here: 265 us
  blocking collectives  73.2 us (27%)
  other arithmetic  66.8 us (25%)
  matrix products  45.7 us (17%)
  local copies, waits for them, and re-layouts  30.2 us (11%)
  Pallas kernels  21.6 us (8%)
  between operations  15.4 us (6%)
  starting transfers between devices  11.9 us (4%)
    convert_element_type x1, other arithmetic, shards(): return (attended + mixed).astype(jnp.bfloat16)  29.8 us
    all_gather x1, blocking collectives, shards(): define_side = lambda sheet: jnp.sum(lax.all_gather(sheet, SEQ), axis=0)  26.8 us
    all_gather x1, blocking collectives, side_by_side(): lax.all_gather(both, axis, axis=dim, tiled=True)  25.1 us
    unnamed x5, Pallas kernels  21.6 us
    pmax x3, blocking collectives, by_axis(): return functools.reduce(lax.pmax, axes, shard)  21.3 us
    dot_general x6, matrix products, newton(): inner_term = 13.0 * eye_matrix - jnp.dot(product, inner_term)  13.5 us
    convert_element_type x3, local copies, waits for them, and re-layouts, dequant(): value_rows.reshape(value_rows.shape[0], count, HEAD_DIM).astype(jnp.float32)  11.9 us
    sub x1, other arithmetic, shards(): local_term = jax.nn.softmax(near_scores, axis=-1).astype(jnp.bfloat16)  11.7 us
  transfers between devices with their start and end apart: 4, of which 0 were waited for; matrix products, arithmetic and copies ran while one was open for 33% of the time, Pallas kernels for 8%

profile of v1, /device:TPU:32, one launch (start us, length us, event | category | flops | bytes accessed | tf_op | source)
XLA Modules:
  0.0 264.9 jit_solution(17511866037577358979)
XLA Ops:
  6.5 4.8 %reshape.134 = f32[8,256,4,128]{3,2,1,0:T(4,128)} reshape(bf16[2048,512]{1,0:T(8,128)(2,1)} %param.7) | data formatting | bytes 6291456 | tf_op jit(solution)/shard_map/convert_element_type | solution.py:61
  11.7 4.6 %convert_reduce_fusion.1 = f32[8,4,128]{2,1,0:T(4,128)S(1)} fusion(f32[8,256,4,128]{3,2,1,0:T(4,128)} %reshape.134, f32[8,256,4]{2,1,0:T(8,128)S(1)} %bitcast.121), kind=kLoop, calls=%fused_computation.52 | loop fusion | flops 4190208 | bytes 4243456 | tf_op jit(solution)/shard_map/reduce_sum | solution.py:90
  16.3 3.0 %reshape.135 = f32[8,256,4,128]{3,2,1,0:T(4,128)} reshape(bf16[2048,512]{1,0:T(8,128)(2,1)S(1)} %copy-done.4) | data formatting | bytes 6291456 | tf_op jit(solution)/shard_map/convert_element_type | solution.py:61
  19.6 4.4 %convert_reduce_fusion = f32[8,4,128]{2,1,0:T(4,128)S(1)} fusion(f32[8,256,4,128]{3,2,1,0:T(4,128)} %reshape.135, f32[8,256,4]{2,1,0:T(8,128)S(1)} %bitcast.122), kind=kLoop, calls=%fused_computation.50 | loop fusion | flops 4190208 | bytes 4243456 | tf_op jit(solution)/shard_map/reduce_sum | solution.py:90
  24.1 25.1 %all_gather.7 = bf16[256,1024]{1,0:T(8,128)(2,1)S(1)} all-gather(bf16[8,1024]{1,0:T(8,128)(2,1)S(1)} %pad_maximum_fusion.2), channel_id=1, replica_groups=mesh['seq_0'=4,'seq_1'=4,'seq_2'=2,'head'=8] {'seq_0','seq_1','seq_2'}, dimensions={0}, use_global_device_ids=true | all-gather | bytes 540672 | tf_op jit(solution)/shard_map/all_gather | solution.py:16
  49.3 0.8 copy.112
  50.2 1.4 fusion.169
  53.1 0.7 reduce_max.56
  53.8 1.3 pad_maximum_fusion.3
  55.7 8.6 %all-to-all-start = ((f32[8,1,2]{2,1,0:T(1,128)}), f32[8,1,2]{2,1,0:T(1,128)S(1)}, u32[]{:S(2)}, u32[]{:S(2)}) async-start(f32[8,1,2]{2,1,0:T(1,128)} %broadcast_in_dim.4), calls=%async_computation | async-start | bytes 8192 | tf_op jit(solution)/shard_map/all_to_all | solution.py:25
  64.3 4.4 %multiply_reduce_fusion = (f32[4,256]{1,0:T(4,128)S(1)}, f32[4,256,2048]{2,1,0:T(8,128)}) fusion(bf16[256,4,128]{0,2,1:T(8,128)(2,1)S(1)} %bitcast.125, f32[2048,4]{0,1:T(4,128)S(1)} %copy-done.11, bf16[2048,512]{1,0:T(8,128)(2,1)S(1)} %copy-done.4), kind=kOutput, calls=%fused_computation.34 | convolution fusion | flops 544209920 | bytes 10784768 | tf_op jit(solution)/shard_map/kli,nli->lkn/dot_general | solution.py:109
  68.7 10.2 %pmax.21 = f32[4,256]{1,0:T(4,128)S(1)} all-reduce(f32[4,256]{1,0:T(4,128)S(1)} %get-tuple-element.48), channel_id=1, replica_groups=mesh['seq_0'=4,'seq_1'=4,'seq_2'=2,'head'=8] {'seq_0'}, use_global_device_ids=true, to_apply=%region_10.0 | all-reduce | flops 1024 | bytes 8192 | tf_op jit(solution)/shard_map/pmax | solution.py:43
  78.9 8.6 %pmax.22 = f32[4,256]{1,0:T(4,128)S(1)} all-reduce(f32[4,256]{1,0:T(4,128)S(1)} %pmax.21), channel_id=1, replica_groups=mesh['seq_0'=4,'seq_1'=4,'seq_2'=2,'head'=8] {'seq_1'}, use_global_device_ids=true, to_apply=%region_11.0 | all-reduce | flops 1024 | bytes 8192 | tf_op jit(solution)/shard_map/pmax | solution.py:43
  87.5 2.5 pmax.23
  89.9 4.2 %copy.106 = f32[2048,512]{0,1:T(8,128)} copy(bf16[2048,512]{1,0:T(8,128)(2,1)} %param.9) | data formatting | bytes 6291456 | tf_op jit(solution)/shard_map/convert_element_type | solution.py:61
  94.1 2.7 %multiply_convert_fusion.1 = bf16[2048,4,128]{0,2,1:T(8,128)(2,1)S(1)} fusion(f32[2048,4,128]{0,2,1:T(8,128)} %bitcast.119, f32[2048,4]{0,1:T(4,128)S(1)} %copy-done.10), kind=kLoop, calls=%fused_computation.49 | loop fusion | flops 2097152 | bytes 6324224 | tf_op jit(solution)/shard_map/convert_element_type | solution.py:62
  96.8 5.9 %fusion.121 = bf16[256,4,128]{0,2,1:T(8,128)(2,1)} fusion(bf16[2048,4,128]{0,2,1:T(8,128)(2,1)S(1)} %multiply_convert_fusion.1, f32[4,256,2048]{2,1,0:T(8,128)} %get-tuple-element.49, f32[4,256]{1,0:T(4,128)S(1)} %pmax.23), kind=kOutput, calls=%fused_computation.148 | convolution fusion | flops 543293440 | bytes 10752000 | tf_op jit(solution)/shard_map/lnx,xlj->nlj/dot_general | solution.py:115
  102.9 2.1 collective-permute-start
  105.1 1.3 collective-permute-start.1
  106.4 4.4 %fusion.2 = bf16[4,256]{1,0:T(4,128)(2,1)S(1)} fusion(f32[4,256,2048]{2,1,0:T(8,128)} %get-tuple-element.49, f32[4,256]{1,0:T(4,128)S(1)} %pmax.23), kind=kLoop, calls=%fused_computation.37 | loop fusion | flops 6290432 | bytes 8394752 | tf_op jit(solution)/shard_map/reduce_sum | solution.py:114
  110.9 4.2 %fusion.16 = f32[4,2048,256]{1,2,0:T(8,128)} fusion(bf16[256,4,128]{0,2,1:T(8,128)(2,1)S(1)} %bitcast.127, f32[2048,4]{0,1:T(4,128)S(1)} %copy-done.12, bf16[2048,512]{1,0:T(8,128)(2,1)S(1)} %copy-done.5), kind=kOutput, calls=%fused_computation.56 | convolution fusion | flops 540016640 | bytes 10780672 | tf_op jit(solution)/shard_map/zea,uea->ezu/dot_general | solution.py:129
  115.4 0.7 fusion.166
  116.1 0.7 fusion.167
  116.7 26.8 %all-gather.1 = bf16[32,4,256]{2,1,0:T(4,128)(2,1)S(1)} all-gather(bf16[1,4,256]{2,1,0:T(4,128)(2,1)S(1)} %bitcast.166), channel_id=2, replica_groups=mesh['seq_0'=4,'seq_1'=4,'seq_2'=2,'head'=8] {'seq_0','seq_1','seq_2'}, dimensions={0}, use_global_device_ids=true | all-gather | bytes 67584 | tf_op jit(solution)/shard_map/all_gather | solution.py:121
  144.2 11.7 %fusion.170 = (f32[4,2048]{1,0:T(4,128)S(1)}, f32[4,2048,256]{1,2,0:T(8,128)}) fusion(f32[4,2048,256]{1,2,0:T(8,128)} %fusion.16), kind=kOutput, calls=%fused_computation.200 | output fusion | flops 8388863 | bytes 16809984 | tf_op jit(solution)/shard_map/sub | solution.py:132
  155.9 2.5 mul.490
  158.4 5.3 %copy.108 = f32[2048,512]{1,0:T(8,128)} copy(f32[2048,512]{0,1:T(8,128)} %bitcast.120) | data formatting | bytes 8388608 | tf_op jit(solution)/shard_map/mul | solution.py:62
  163.7 4.9 %multiply_convert_fusion = bf16[2048,512]{1,0:T(8,128)(2,1)} fusion(f32[2048,512]{1,0:T(8,128)} %copy.108, bf16[2048,512]{1,0:T(8,128)(2,1)} %param.9), kind=kLoop, calls=%fused_computation.45 | loop fusion | flops 3145728 | bytes 8388608 | tf_op jit(solution)/shard_map/convert_element_type | solution.py:62
  170.5 1.4 fusion.150
  172.4 1.8 convolution_multiply_fusion.5
  174.2 4.3 %online-softmax = f32[4,256,256]{2,1,0:T(8,128)} custom-call(f32[4,256,256]{2,1,0:T(8,128)} %copy-done, f32[4,256,256]{2,1,0:T(8,128)} %convolution_multiply_fusion.5), custom_call_target="tpu_custom_call" | custom-call | tf_op online-softmax
  178.5 2.6 fusion.77
  181.1 1.4 convolution_multiply_fusion.4
  182.5 4.3 %online-softmax.1 = f32[4,256,256]{2,1,0:T(8,128)} custom-call(f32[4,256,256]{2,1,0:T(8,128)} %copy-done, f32[4,256,256]{2,1,0:T(8,128)} %convolution_multiply_fusion.4), custom_call_target="tpu_custom_call" | custom-call | tf_op online-softmax
  186.8 2.6 fusion.86
  189.4 1.4 convolution_multiply_fusion.3
  190.8 4.3 %online-softmax.2 = f32[4,256,256]{2,1,0:T(8,128)} custom-call(f32[4,256,256]{2,1,0:T(8,128)} %copy-done, f32[4,256,256]{2,1,0:T(8,128)} %convolution_multiply_fusion.3), custom_call_target="tpu_custom_call" | custom-call | tf_op online-softmax
  195.1 2.6 fusion.95
  197.7 1.4 convolution_multiply_fusion.2
  199.1 4.3 %online-softmax.3 = f32[4,256,256]{2,1,0:T(8,128)} custom-call(f32[4,256,256]{2,1,0:T(8,128)} %copy-done, f32[4,256,256]{2,1,0:T(8,128)} %convolution_multiply_fusion.2), custom_call_target="tpu_custom_call" | custom-call | tf_op online-softmax
  203.4 2.6 fusion.104
  206.0 1.4 convolution_multiply_fusion.1
  207.4 4.3 %online-softmax.4 = f32[4,256,256]{2,1,0:T(8,128)} custom-call(f32[4,256,256]{2,1,0:T(8,128)} %copy-done, f32[4,256,256]{2,1,0:T(8,128)} %convolution_multiply_fusion.1), custom_call_target="tpu_custom_call" | custom-call | tf_op online-softmax
  211.7 2.6 fusion.113
  214.4 1.4 fusion.124
  215.8 6.2 %fusion.13 = f32[4,128,2048]{2,1,0:T(8,128)} fusion(bf16[256,4,128]{2,0,1:T(8,128)(2,1)S(1)} %fusion.124, f32[4,2048,256]{1,2,0:T(8,128)} %get-tuple-element.51, f32[4,2048]{1,0:T(4,128)S(1)} %get-tuple-element.50), kind=kOutput, calls=%fused_computation.54 | convolution fusion | flops 541065216 | bytes 12877824 | tf_op jit(solution)/shard_map/kbv,vkg->bkg/dot_general | solution.py:133
  222.3 5.5 %copy.94 = f32[2048,512]{1,0:T(8,128)} copy(f32[2048,512]{0,1:T(8,128)} %bitcast.123) | data formatting | bytes 8388608 | tf_op jit(solution)/shard_map/reshape | solution.py:135
  228.2 29.8 %add_convert_fusion = bf16[2048,512]{1,0:T(8,128)(2,1)} fusion(f32[2048,512]{1,0:T(8,128)} %copy.94, bf16[2048,512]{1,0:T(8,128)(2,1)S(1)} %copy-done.6, bf16[16,512]{1,0:T(8,128)(2,1)S(1)} %collective-permute-done.1, bf16[16,512]{1,0:T(8,128)(2,1)S(1)} %collective-permute-done, f32[512]{0:T(512)S(1)} %bitcast.134, f32[512]{0:T(512)S(1)} %bitcast.135, ...), kind=kLoop, calls=%fused_computation.44 | loop fusion | flops 205520896 | bytes 8488960 | tf_op jit(solution)/shard_map/convert_element_type | solution.py:146
  (127 shorter events, 5.6 us)
Async XLA Ops:
  6.5 4.8 %copy-start.12 = (f32[2048,4]{0,1:T(4,128)S(1)}, f32[2048,4]{0,1:T(4,128)}, u32[]{:S(2)}) copy-start(f32[2048,4]{0,1:T(4,128)} %param.10) | copy-start | bytes 98308
  11.3 5.0 %copy-start.4 = (bf16[2048,512]{1,0:T(8,128)(2,1)S(1)}, bf16[2048,512]{1,0:T(8,128)(2,1)}, u32[]{:S(2)}) copy-start(bf16[2048,512]{1,0:T(8,128)(2,1)} %param.8) | copy-start | bytes 6291460
  51.6 120.8 %copy-start = (f32[4,256,256]{2,1,0:T(8,128)}, f32[4,256,256]{2,1,0:T(8,128)S(1)}, u32[]{:S(2)}) copy-start(f32[4,256,256]{2,1,0:T(8,128)S(1)} %get-tuple-element.47) | copy-start | bytes 3145732
  55.7 112.9 %all-to-all-start = ((f32[8,1,2]{2,1,0:T(1,128)}), f32[8,1,2]{2,1,0:T(1,128)S(1)}, u32[]{:S(2)}, u32[]{:S(2)}) async-start(f32[8,1,2]{2,1,0:T(1,128)} %broadcast_in_dim.4), calls=%async_computation | async-start | bytes 8192 | tf_op jit(solution)/shard_map/all_to_all | solution.py:25
  64.3 150.1 %all-reduce.2.cloned.1.call-start = ((), (), s32[]{:S(2)}) async-start(), calls=%async_computation.1 | async-start | bytes 524288 | tf_op jit(solution)/shard_map/psum | solution.py:124
  68.7 25.4 %copy-start.10 = (f32[2048,4]{0,1:T(4,128)S(1)}, f32[2048,4]{0,1:T(4,128)}, u32[]{:S(2)}) copy-start(f32[2048,4]{0,1:T(4,128)} %param.12) | copy-start | bytes 98308
  102.9 124.9 %collective-permute-start = (bf16[16,512]{1,0:T(8,128)(2,1)S(1)}, bf16[16,512]{1,0:T(8,128)(2,1)S(1)}, u32[]{:S(2)}, u32[]{:S(2)}) collective-permute-start(bf16[16,512]{1,0:T(8,128)(2,1)S(1)} %copy.107), channel_id=1, source_target_pairs={{0,8},{8,16},{16,24},{24,32},{32,40},{40,48},{48,56},{56,64},{64,7... | collective-permute-start | bytes 49160 | tf_op jit(solution)/shard_map/ppermute | solution.py:53
  105.1 122.8 %collective-permute-start.1 = (bf16[16,512]{1,0:T(8,128)(2,1)S(1)}, bf16[16,512]{1,0:T(8,128)(2,1)S(1)}, u32[]{:S(2)}, u32[]{:S(2)}) collective-permute-start(bf16[16,512]{1,0:T(8,128)(2,1)S(1)} %copy.109), channel_id=1, source_target_pairs={{8,0},{16,8},{24,16},{32,24},{40,32},{48,40},{56,48},{64,56},{72,6... | collective-permute-start | bytes 49160 | tf_op jit(solution)/shard_map/ppermute | solution.py:54
  106.4 4.5 %copy-start.5 = (bf16[2048,512]{1,0:T(8,128)(2,1)S(1)}, bf16[2048,512]{1,0:T(8,128)(2,1)}, u32[]{:S(2)}) copy-start(bf16[2048,512]{1,0:T(8,128)(2,1)} %param.7) | copy-start | bytes 6291460
  174.2 6.9 %copy-start.8 = (f32[4,256,256]{2,1,0:T(8,128)S(1)}, f32[4,256,256]{2,1,0:T(8,128)}, u32[]{:S(2)}) copy-start(f32[4,256,256]{2,1,0:T(8,128)} %convolution_multiply_fusion.5) | copy-start | bytes 3145732
  182.5 6.9 %copy-start.1 = (f32[4,256,256]{2,1,0:T(8,128)S(1)}, f32[4,256,256]{2,1,0:T(8,128)}, u32[]{:S(2)}) copy-start(f32[4,256,256]{2,1,0:T(8,128)} %convolution_multiply_fusion.4) | copy-start | bytes 3145732
  190.8 6.9 %copy-start.2 = (f32[4,256,256]{2,1,0:T(8,128)S(1)}, f32[4,256,256]{2,1,0:T(8,128)}, u32[]{:S(2)}) copy-start(f32[4,256,256]{2,1,0:T(8,128)} %convolution_multiply_fusion.3) | copy-start | bytes 3145732
  199.1 6.9 %copy-start.3 = (f32[4,256,256]{2,1,0:T(8,128)S(1)}, f32[4,256,256]{2,1,0:T(8,128)}, u32[]{:S(2)}) copy-start(f32[4,256,256]{2,1,0:T(8,128)} %convolution_multiply_fusion.2) | copy-start | bytes 3145732
  207.4 6.9 %copy-start.7 = (f32[4,256,256]{2,1,0:T(8,128)S(1)}, f32[4,256,256]{2,1,0:T(8,128)}, u32[]{:S(2)}) copy-start(f32[4,256,256]{2,1,0:T(8,128)} %convolution_multiply_fusion.1) | copy-start | bytes 3145732
  207.4 7.0 %copy-start.45 = (f32[256,4]{0,1:T(4,128)S(1)}, f32[256,4]{0,1:T(4,128)}, u32[]{:S(2)}) copy-start(f32[256,4]{0,1:T(4,128)} %convert_bitcast_fusion.2) | copy-start | bytes 12292
  222.0 5.8 %copy-start.6 = (bf16[2048,512]{1,0:T(8,128)(2,1)S(1)}, bf16[2048,512]{1,0:T(8,128)(2,1)}, u32[]{:S(2)}) copy-start(bf16[2048,512]{1,0:T(8,128)(2,1)} %multiply_convert_fusion) | copy-start | bytes 6291460
  222.0 5.8 %copy-start.13 = (f32[512,1]{0,1:T(1,128)S(1)}, f32[512,1]{0,1:T(1,128)}, u32[]{:S(2)}) copy-start(f32[512,1]{0,1:T(1,128)} %get-tuple-element.12) | copy-start | bytes 6148
  222.0 5.9 %copy-start.14 = (f32[512,1]{0,1:T(1,128)S(1)}, f32[512,1]{0,1:T(1,128)}, u32[]{:S(2)}) copy-start(f32[512,1]{0,1:T(1,128)} %get-tuple-element.13) | copy-start | bytes 6148
  222.0 5.9 %copy-start.15 = (f32[512,1]{0,1:T(1,128)S(1)}, f32[512,1]{0,1:T(1,128)}, u32[]{:S(2)}) copy-start(f32[512,1]{0,1:T(1,128)} %get-tuple-element.14) | copy-start | bytes 6148
  222.0 5.9 %copy-start.16 = (f32[512,1]{0,1:T(1,128)S(1)}, f32[512,1]{0,1:T(1,128)}, u32[]{:S(2)}) copy-start(f32[512,1]{0,1:T(1,128)} %get-tuple-element.15) | copy-start | bytes 6148
  222.0 5.9 %copy-start.17 = (f32[512,1]{0,1:T(1,128)S(1)}, f32[512,1]{0,1:T(1,128)}, u32[]{:S(2)}) copy-start(f32[512,1]{0,1:T(1,128)} %get-tuple-element.16) | copy-start | bytes 6148
  222.1 5.9 %copy-start.18 = (f32[512,1]{0,1:T(1,128)S(1)}, f32[512,1]{0,1:T(1,128)}, u32[]{:S(2)}) copy-start(f32[512,1]{0,1:T(1,128)} %get-tuple-element.17) | copy-start | bytes 6148
  222.1 5.9 %copy-start.19 = (f32[512,1]{0,1:T(1,128)S(1)}, f32[512,1]{0,1:T(1,128)}, u32[]{:S(2)}) copy-start(f32[512,1]{0,1:T(1,128)} %get-tuple-element.18) | copy-start | bytes 6148
  222.1 5.9 %copy-start.20 = (f32[512,1]{0,1:T(1,128)S(1)}, f32[512,1]{0,1:T(1,128)}, u32[]{:S(2)}) copy-start(f32[512,1]{0,1:T(1,128)} %get-tuple-element.19) | copy-start | bytes 6148
  222.1 5.9 %copy-start.21 = (f32[512,1]{0,1:T(1,128)S(1)}, f32[512,1]{0,1:T(1,128)}, u32[]{:S(2)}) copy-start(f32[512,1]{0,1:T(1,128)} %get-tuple-element.20) | copy-start | bytes 6148
  222.1 5.9 %copy-start.22 = (f32[512,1]{0,1:T(1,128)S(1)}, f32[512,1]{0,1:T(1,128)}, u32[]{:S(2)}) copy-start(f32[512,1]{0,1:T(1,128)} %get-tuple-element.21) | copy-start | bytes 6148
  222.1 5.9 %copy-start.23 = (f32[512,1]{0,1:T(1,128)S(1)}, f32[512,1]{0,1:T(1,128)}, u32[]{:S(2)}) copy-start(f32[512,1]{0,1:T(1,128)} %get-tuple-element.22) | copy-start | bytes 6148
  222.1 5.9 %copy-start.24 = (f32[512,1]{0,1:T(1,128)S(1)}, f32[512,1]{0,1:T(1,128)}, u32[]{:S(2)}) copy-start(f32[512,1]{0,1:T(1,128)} %get-tuple-element.23) | copy-start | bytes 6148
  222.1 5.9 %copy-start.25 = (f32[512,1]{0,1:T(1,128)S(1)}, f32[512,1]{0,1:T(1,128)}, u32[]{:S(2)}) copy-start(f32[512,1]{0,1:T(1,128)} %get-tuple-element.24) | copy-start | bytes 6148
  222.1 5.9 %copy-start.26 = (f32[512,1]{0,1:T(1,128)S(1)}, f32[512,1]{0,1:T(1,128)}, u32[]{:S(2)}) copy-start(f32[512,1]{0,1:T(1,128)} %get-tuple-element.25) | copy-start | bytes 6148
  222.1 5.9 %copy-start.27 = (f32[512,1]{0,1:T(1,128)S(1)}, f32[512,1]{0,1:T(1,128)}, u32[]{:S(2)}) copy-start(f32[512,1]{0,1:T(1,128)} %get-tuple-element.26) | copy-start | bytes 6148
  222.2 5.9 %copy-start.28 = (f32[512,1]{0,1:T(1,128)S(1)}, f32[512,1]{0,1:T(1,128)}, u32[]{:S(2)}) copy-start(f32[512,1]{0,1:T(1,128)} %get-tuple-element.27) | copy-start | bytes 6148
  222.2 5.9 %copy-start.29 = (f32[512,1]{0,1:T(1,128)S(1)}, f32[512,1]{0,1:T(1,128)}, u32[]{:S(2)}) copy-start(f32[512,1]{0,1:T(1,128)} %get-tuple-element.28) | copy-start | bytes 6148
  222.2 5.9 %copy-start.30 = (f32[512,1]{0,1:T(1,128)S(1)}, f32[512,1]{0,1:T(1,128)}, u32[]{:S(2)}) copy-start(f32[512,1]{0,1:T(1,128)} %get-tuple-element.29) | copy-start | bytes 6148
  222.2 5.9 %copy-start.31 = (f32[512,1]{0,1:T(1,128)S(1)}, f32[512,1]{0,1:T(1,128)}, u32[]{:S(2)}) copy-start(f32[512,1]{0,1:T(1,128)} %get-tuple-element.30) | copy-start | bytes 6148
  222.2 5.9 %copy-start.32 = (f32[512,1]{0,1:T(1,128)S(1)}, f32[512,1]{0,1:T(1,128)}, u32[]{:S(2)}) copy-start(f32[512,1]{0,1:T(1,128)} %get-tuple-element.31) | copy-start | bytes 6148
  222.2 5.9 %copy-start.33 = (f32[512,1]{0,1:T(1,128)S(1)}, f32[512,1]{0,1:T(1,128)}, u32[]{:S(2)}) copy-start(f32[512,1]{0,1:T(1,128)} %get-tuple-element.32) | copy-start | bytes 6148
  222.2 5.9 %copy-start.34 = (f32[512,1]{0,1:T(1,128)S(1)}, f32[512,1]{0,1:T(1,128)}, u32[]{:S(2)}) copy-start(f32[512,1]{0,1:T(1,128)} %get-tuple-element.33) | copy-start | bytes 6148
  222.2 5.9 %copy-start.35 = (f32[512,1]{0,1:T(1,128)S(1)}, f32[512,1]{0,1:T(1,128)}, u32[]{:S(2)}) copy-start(f32[512,1]{0,1:T(1,128)} %get-tuple-element.34) | copy-start | bytes 6148
  222.2 5.9 %copy-start.36 = (f32[512,1]{0,1:T(1,128)S(1)}, f32[512,1]{0,1:T(1,128)}, u32[]{:S(2)}) copy-start(f32[512,1]{0,1:T(1,128)} %get-tuple-element.35) | copy-start | bytes 6148
  222.2 5.9 %copy-start.37 = (f32[512,1]{0,1:T(1,128)S(1)}, f32[512,1]{0,1:T(1,128)}, u32[]{:S(2)}) copy-start(f32[512,1]{0,1:T(1,128)} %get-tuple-element.36) | copy-start | bytes 6148
  222.3 5.9 %copy-start.38 = (f32[512,1]{0,1:T(1,128)S(1)}, f32[512,1]{0,1:T(1,128)}, u32[]{:S(2)}) copy-start(f32[512,1]{0,1:T(1,128)} %get-tuple-element.37) | copy-start | bytes 6148
  222.3 5.9 %copy-start.39 = (f32[512,1]{0,1:T(1,128)S(1)}, f32[512,1]{0,1:T(1,128)}, u32[]{:S(2)}) copy-start(f32[512,1]{0,1:T(1,128)} %get-tuple-element.38) | copy-start | bytes 6148
  222.3 5.9 %copy-start.40 = (f32[512,1]{0,1:T(1,128)S(1)}, f32[512,1]{0,1:T(1,128)}, u32[]{:S(2)}) copy-start(f32[512,1]{0,1:T(1,128)} %get-tuple-element.39) | copy-start | bytes 6148
  222.3 5.9 %copy-start.41 = (f32[512,1]{0,1:T(1,128)S(1)}, f32[512,1]{0,1:T(1,128)}, u32[]{:S(2)}) copy-start(f32[512,1]{0,1:T(1,128)} %get-tuple-element.40) | copy-start | bytes 6148
  222.3 5.9 %copy-start.42 = (f32[512,1]{0,1:T(1,128)S(1)}, f32[512,1]{0,1:T(1,128)}, u32[]{:S(2)}) copy-start(f32[512,1]{0,1:T(1,128)} %get-tuple-element.41) | copy-start | bytes 6148
  222.3 5.9 %copy-start.43 = (f32[512,1]{0,1:T(1,128)S(1)}, f32[512,1]{0,1:T(1,128)}, u32[]{:S(2)}) copy-start(f32[512,1]{0,1:T(1,128)} %get-tuple-element.42) | copy-start | bytes 6148
  222.3 5.9 %copy-start.44 = (f32[512,1]{0,1:T(1,128)S(1)}, f32[512,1]{0,1:T(1,128)}, u32[]{:S(2)}) copy-start(f32[512,1]{0,1:T(1,128)} %get-tuple-element.43) | copy-start | bytes 6148
  (3 other events, 11.8 us)
Sparse Core Ops, SparseCore 0:
  102.9 108.6 all-reduce.1
